TPU v7x, 32 devices: a whole 2x2x4 slice. The times are simulated.
32 devices in a mesh: rows: 8 (over z, x), seq: 4 (over y, core).
Axes of the slice: x: 2, y: 2, z: 4, core: 2. Of those that a mesh axis runs over, the one named last changes fastest.
Arguments:
- frames_in: bfloat16 [16, 4096, 512], P('rows', 'seq'), may hold values from -6 to 6
- lengths: int32 [16, 4], P('rows'), may hold values from 1 to 2048, 4096 in all within a row
- bw_ids: int32 [16, 4], P('rows'), may hold values from 0 to 3
- owner_list: int32 [137], replicated, may hold values from 0 to 7, as said below
- master: float32 [216, 32, 512], P('rows')
- moment1: float32 [216, 32, 512], P('rows')
- moment2: float32 [216, 32, 512], P('rows'), as said below
- wave_grad: bfloat16 [16, 1310720], P('rows', 'seq'), may hold values from -6 to 6
Outputs:
- waveform: float32 [16, 1310720], P('rows', 'seq')
- input_grad: float32 [16, 4096, 512], P('rows', 'seq')
- new_master: float32 [216, 32, 512], P('rows')
- new_moment1: float32 [216, 32, 512], P('rows')
- new_moment2: float32 [216, 32, 512], P('rows')
Inputs may be any that keep to these rules, and one draw needn't show every extreme that they name: `owner_list`: no index along rows owns more than 27 buckets, and some index owns exactly 27. `moment2`: every entry is positive.
All inputs are finite; a program needn't handle non-finite values.
Results may differ from a plain program's by a relative error of at most 0.012.
The roundings to bfloat16 on the way count: a program that leaves them out, or rounds other values in their place, can miss the bound.
Values may be sent and summed in bfloat16 or wider, within the bound.
No kernel may reach another device: no remote copies, remote signals or barrier semaphores. Data moves between devices by JAX's collectives and lax.ppermute only.
A program may use at most 192 MiB of HBM per device.

v0:
```python
import math
import jax
import jax.numpy as jnp
from jax import lax
from jax.sharding import PartitionSpec as P

FF = 1536
NFFT = 1280
HOP = 320
NBW = 4
KW = 7
UTT = 4
BR = 32
STEP_COUNT = 6
BINS = 641
NOUT = 1282
VROWS = 20
IN_ROWS = 3
HEAD_ROWS = 3
PR = 4380
NB = 137
NORM_EPS = 1e-06
ENV_FLOOR = 0.5
BETA_ONE = 0.8
BETA_TWO = 0.9
LEARN_RATE = 0.04
WEIGHT_DECAY = 0.01
ADAM_EPS = 1e-08


def padded(block, sides, width):
    for axis, dim in sides:
        count = lax.axis_size(axis)
        forward = [(i, i + 1) for i in range(count - 1)]
        backward = [(target, source) for source, target in forward]
        low = lax.ppermute(
            lax.slice_in_dim(block, block.shape[dim] - width, None, axis=dim), axis, forward
        )
        high = lax.ppermute(lax.slice_in_dim(block, 0, width, axis=dim), axis, backward)
        block = jnp.concatenate([low, block, high], axis=dim)
    return block


def from_behind(block, axis, distance):
    devices = range(lax.axis_size(axis))
    route = [(i - distance, i) for i in devices if i - distance in devices]
    return lax.ppermute(block, axis, route)


def slot_maps(owner_list, owner_count, slot_count):
    bucket_count = owner_list.shape[0]
    bucket_index = jnp.arange(bucket_count, dtype=jnp.int32)
    same_owner = owner_list[None, :] == owner_list[:, None]
    before = bucket_index[None, :] < bucket_index[:, None]
    slot_rank = jnp.sum((same_owner & before).astype(jnp.int32), axis=1)
    bucket_place = owner_list * slot_count + slot_rank
    targets = jnp.arange(owner_count * slot_count, dtype=jnp.int32)
    slot_match = bucket_place[None, :] == targets[:, None]
    found_bucket = jnp.sum(slot_match.astype(jnp.int32) * bucket_index[None, :], axis=1)
    source = jnp.where(jnp.any(slot_match, axis=1), found_bucket, bucket_count)
    return (bucket_place, source)


def synthesis_table():
    bin_index = jnp.arange(BINS, dtype=jnp.int32)[:, None]
    tap_index = jnp.arange(NFFT, dtype=jnp.int32)[None, :]
    turns = bin_index * tap_index % NFFT
    angle = turns.astype(jnp.float32) * (2.0 * math.pi / NFFT)
    edge_bin = (bin_index == 0) | (bin_index == NFFT // 2)
    factor = jnp.where(edge_bin, 1.0, 2.0).astype(jnp.float32) / NFFT
    return jnp.concatenate([factor * jnp.cos(angle), -factor * jnp.sin(angle)], axis=0)


def hann_window():
    angle = jnp.arange(NFFT, dtype=jnp.int32).astype(jnp.float32) * (2.0 * math.pi / NFFT)
    return 0.5 - 0.5 * jnp.cos(angle)


def segment_ids(lengths, first_index, span):
    starts = jnp.cumsum(lengths, axis=1) - lengths
    frame_index = first_index + jnp.arange(span, dtype=jnp.int32)
    return jnp.sum((starts[:, None, :] <= frame_index[None, :, None]).astype(jnp.int32), axis=2) - 1


def layer_norm(values):
    row_mean = jnp.mean(values, axis=-1, keepdims=True)
    centered = values - row_mean
    return centered * lax.rsqrt(jnp.mean(centered * centered, axis=-1, keepdims=True) + NORM_EPS)


def ada_norm(values, scale_rows, shift_rows):
    return layer_norm(values) * scale_rows + shift_rows


def final_norm(values, norm_gain, norm_bias):
    return layer_norm(values) * norm_gain[None, :] + norm_bias[None, :]


def exact_gelu(values):
    return jax.nn.gelu(values, approximate=False)


def contract(left_side, right_side, left_dim, right_dim):
    return lax.dot_general(
        left_side,
        right_side,
        (((left_dim,), (right_dim,)), ((), ())),
        preferred_element_type=jnp.float32,
    )


def local(frames_in, lengths, bw_ids, owner_list, master, moment1, moment2, wave_grad):
    rows_here, frames_here, channels = frames_in.shape
    slot_count = master.shape[0]
    frame_count = rows_here * frames_here
    lap_count = NFFT // HOP
    rim_width = (KW - 1) // 2
    margin = max(rim_width, lap_count - 1)
    bucket_place, source = slot_maps(owner_list, lax.axis_size("rows"), slot_count)
    gathered = lax.all_gather(master.astype(jnp.bfloat16), "rows", axis=0, tiled=True)
    buckets = jnp.take(gathered, bucket_place, axis=0)
    weight_table = buckets.reshape(-1, channels)[:PR]
    w_in = weight_table[:FF]
    w_out = weight_table[FF : 2 * FF]
    w_head = weight_table[2 * FF : 2 * FF + NOUT]
    row_start = 2 * FF + NOUT
    channel_rows = weight_table[row_start : row_start + VROWS].astype(jnp.float32)
    row_start = row_start + VROWS
    bias_in = weight_table[row_start : row_start + IN_ROWS].reshape(-1).astype(jnp.float32)
    row_start = row_start + IN_ROWS
    bias_head = (
        weight_table[row_start : row_start + HEAD_ROWS].reshape(-1)[:NOUT].astype(jnp.float32)
    )
    conv_weight = channel_rows[:KW]
    conv_bias = channel_rows[KW]
    ada_scale = channel_rows[KW + 1 : KW + 1 + NBW]
    ada_shift = channel_rows[KW + 1 + NBW : KW + 1 + 2 * NBW]
    vec_base = KW + 1 + 2 * NBW
    bias_out = channel_rows[vec_base]
    layer_scale = channel_rows[vec_base + 1]
    norm_gain = channel_rows[vec_base + 2]
    norm_bias = channel_rows[vec_base + 3]
    first_index = lax.axis_index("seq") * frames_here - margin
    segment = segment_ids(lengths, first_index, frames_here + 2 * margin)
    own_segment = segment[:, margin : margin + frames_here]
    halo_frames = padded(frames_in, (("seq", 1),), rim_width)
    wide_frames = halo_frames.astype(jnp.float32)
    conv_keep = []
    conv_out = jnp.zeros((rows_here, frames_here, channels), jnp.float32) + conv_bias
    for tap_index in range(KW):
        lower = margin - rim_width + tap_index
        keep = (segment[:, lower : lower + frames_here] == own_segment).astype(jnp.float32)[
            :, :, None
        ]
        conv_keep.append(keep)
        conv_out = (
            conv_out
            + keep * wide_frames[:, tap_index : tap_index + frames_here] * conv_weight[tap_index]
        )
    conv_out = conv_out.reshape(frame_count, channels)
    utt_pick = (own_segment[:, :, None] == jnp.arange(UTT, dtype=jnp.int32)[None, None, :]).astype(
        jnp.int32
    )
    frame_ids = jnp.sum(utt_pick * bw_ids[:, None, :], axis=2).reshape(frame_count)
    bw_onehot = (frame_ids[:, None] == jnp.arange(NBW, dtype=jnp.int32)[None, :]).astype(
        jnp.float32
    )
    scale_rows = jnp.dot(bw_onehot, ada_scale, precision=lax.Precision.HIGHEST)
    shift_rows = jnp.dot(bw_onehot, ada_shift, precision=lax.Precision.HIGHEST)
    ada_value, ada_back = jax.vjp(ada_norm, conv_out, scale_rows, shift_rows)
    ada_low = ada_value.astype(jnp.bfloat16)
    hidden_pre = contract(ada_low, w_in, 1, 1) + bias_in[None, :]
    act_value, gelu_back = jax.vjp(exact_gelu, hidden_pre)
    act_low = act_value.astype(jnp.bfloat16)
    branch = contract(act_low, w_out, 1, 0) + bias_out[None, :]
    frames_flat = frames_in.reshape(frame_count, channels).astype(jnp.float32)
    residual = frames_flat + layer_scale[None, :] * branch
    normed_value, final_back = jax.vjp(final_norm, residual, norm_gain, norm_bias)
    normed_low = normed_value.astype(jnp.bfloat16)
    head_out = contract(normed_low, w_head, 1, 1) + bias_head[None, :]
    magnitude = jnp.exp(head_out[:, :BINS])
    phase_angle = head_out[:, BINS:]
    real_part = magnitude * jnp.cos(phase_angle)
    imag_part = magnitude * jnp.sin(phase_angle)
    spectrum_low = jnp.concatenate([real_part, imag_part], axis=1).astype(jnp.bfloat16)
    synthesis = synthesis_table().astype(jnp.bfloat16)
    signal = contract(spectrum_low, synthesis, 1, 0)
    window_rows = hann_window().reshape(lap_count, HOP)
    pieces = signal.reshape(rows_here, frames_here, lap_count, HOP) * window_rows[None, None, :, :]
    lap_keep = []
    numerator = jnp.zeros((rows_here, frames_here + lap_count - 1, HOP), jnp.float32)
    envelope = jnp.zeros((rows_here, frames_here, HOP), jnp.float32)
    for lap_index in range(lap_count):
        ahead = margin + lap_index
        keep = (segment[:, ahead : ahead + frames_here] == own_segment).astype(jnp.float32)[
            :, :, None
        ]
        lap_keep.append(keep)
        numerator = numerator + jnp.pad(
            keep * pieces[:, :, lap_index], ((0, 0), (lap_index, lap_count - 1 - lap_index), (0, 0))
        )
        behind = margin - lap_index
        back_keep = (segment[:, behind : behind + frames_here] == own_segment).astype(jnp.float32)[
            :, :, None
        ]
        envelope = envelope + back_keep * (window_rows[lap_index] ** 2)[None, None, :]
    arrived = from_behind(numerator[:, frames_here:], "seq", 1)
    numerator = numerator[:, :frames_here] + jnp.pad(
        arrived, ((0, 0), (0, frames_here - lap_count + 1), (0, 0))
    )
    denominator = jnp.maximum(envelope, ENV_FLOOR)
    waveform = (numerator / denominator).reshape(rows_here, frames_here * HOP)
    scaled = wave_grad.astype(jnp.float32).reshape(rows_here, frames_here, HOP) / denominator
    later_rows = from_behind(scaled[:, : lap_count - 1], "seq", -1)
    reach_rows = jnp.concatenate([scaled, later_rows], axis=1)
    signal_grad = jnp.stack(
        [
            lap_keep[lap_index]
            * window_rows[lap_index][None, None, :]
            * reach_rows[:, lap_index : lap_index + frames_here]
            for lap_index in range(lap_count)
        ],
        axis=2,
    )
    signal_low = signal_grad.reshape(frame_count, NFFT).astype(jnp.bfloat16)
    spec_grad = contract(signal_low, synthesis, 1, 1)
    real_grad = spec_grad[:, :BINS]
    imag_grad = spec_grad[:, BINS:]
    head_grad = jnp.concatenate(
        [
            real_grad * real_part + imag_grad * imag_part,
            imag_grad * real_part - real_grad * imag_part,
        ],
        axis=1,
    ).astype(jnp.bfloat16)
    grad_w_head = contract(head_grad, normed_low, 0, 0)
    grad_b_head = jnp.sum(head_grad, axis=0, dtype=jnp.float32)
    normed_grad = contract(head_grad, w_head, 1, 0)
    residual_grad, grad_gain, grad_bias = final_back(normed_grad)
    branch_low = (layer_scale[None, :] * residual_grad).astype(jnp.bfloat16)
    grad_layer_scale = jnp.sum(residual_grad * branch, axis=0)
    grad_w_out = contract(act_low, branch_low, 0, 0)
    grad_b_out = jnp.sum(branch_low, axis=0, dtype=jnp.float32)
    act_grad = contract(branch_low, w_out, 1, 1)
    pre_low = gelu_back(act_grad)[0].astype(jnp.bfloat16)
    grad_w_in = contract(pre_low, ada_low, 0, 0)
    grad_b_in = jnp.sum(pre_low, axis=0, dtype=jnp.float32)
    ada_grad = contract(pre_low, w_in, 1, 0)
    conv_grad, scale_grad_rows, shift_grad_rows = ada_back(ada_grad)
    grad_scales = lax.dot_general(
        bw_onehot, scale_grad_rows, (((0,), (0,)), ((), ())), precision=lax.Precision.HIGHEST
    )
    grad_shifts = lax.dot_general(
        bw_onehot, shift_grad_rows, (((0,), (0,)), ((), ())), precision=lax.Precision.HIGHEST
    )
    conv_rows = conv_grad.reshape(rows_here, frames_here, channels)
    grad_conv_b = jnp.sum(conv_grad, axis=0)
    grad_conv_w = jnp.stack(
        [
            jnp.sum(
                conv_keep[tap_index]
                * conv_rows
                * wide_frames[:, tap_index : tap_index + frames_here],
                axis=(0, 1),
            )
            for tap_index in range(KW)
        ],
        axis=0,
    )
    halo_grad = padded(conv_rows, (("seq", 1),), rim_width)
    input_grad = residual_grad.reshape(rows_here, frames_here, channels)
    for tap_index in range(KW):
        lower = margin + rim_width - tap_index
        keep = (segment[:, lower : lower + frames_here] == own_segment).astype(jnp.float32)[
            :, :, None
        ]
        begin = 2 * rim_width - tap_index
        input_grad = (
            input_grad + conv_weight[tap_index] * keep * halo_grad[:, begin : begin + frames_here]
        )
    vec_grads = jnp.concatenate(
        [
            grad_conv_w,
            grad_conv_b[None, :],
            grad_scales,
            grad_shifts,
            jnp.stack([grad_b_out, grad_layer_scale, grad_gain, grad_bias], axis=0),
        ],
        axis=0,
    )
    in_rows = grad_b_in.reshape(IN_ROWS, channels)
    head_rows = jnp.pad(grad_b_head, (0, HEAD_ROWS * channels - NOUT)).reshape(HEAD_ROWS, channels)
    grad_table = jnp.concatenate(
        [grad_w_in, grad_w_out, grad_w_head, vec_grads, in_rows, head_rows], axis=0
    )
    grad_buckets = jnp.pad(grad_table, ((0, NB * BR - PR), (0, 0))).reshape(NB, BR, channels)
    empty_bucket = jnp.zeros((1, BR, channels), jnp.float32)
    summed = lax.psum(grad_buckets, ("rows", "seq"))
    extended = jnp.concatenate([summed, empty_bucket], axis=0)
    my_sources = lax.dynamic_slice_in_dim(source, lax.axis_index("rows") * slot_count, slot_count)
    reduced = jnp.take(extended, my_sources, axis=0)
    first_new = BETA_ONE * moment1 + (1.0 - BETA_ONE) * reduced
    second_new = BETA_TWO * moment2 + (1.0 - BETA_TWO) * reduced * reduced
    first_fix = 1.0 - BETA_ONE**STEP_COUNT
    second_fix = 1.0 - BETA_TWO**STEP_COUNT
    master_new = master - LEARN_RATE * (
        first_new / first_fix / (jnp.sqrt(second_new / second_fix) + ADAM_EPS)
        + WEIGHT_DECAY * master
    )
    return (waveform, input_grad, master_new, first_new, second_new)


def solution(mesh):
    in_specs = (
        P("rows", "seq", None),
        P("rows", None),
        P("rows", None),
        P(),
        P("rows", None, None),
        P("rows", None, None),
        P("rows", None, None),
        P("rows", "seq"),
    )
    out_specs = (
        P("rows", "seq"),
        P("rows", "seq", None),
        P("rows", None, None),
        P("rows", None, None),
        P("rows", None, None),
    )
    return jax.shard_map(local, mesh=mesh, in_specs=in_specs, out_specs=out_specs, check_vma=False)
```

profile of v0, /device:TPU:0, one launch (start us, length us, event | category | flops | bytes accessed | tf_op | source)
XLA Modules:
  0.0 546.3 jit_solution(15566940357598605938)
XLA Ops:
  7.2 2.5 convert_element_type.160
  10.6 2.4 collective-permute-start
  12.9 1.3 collective-permute-start.1
  15.8 2.7 reshape.271
  18.5 2.2 copy.39
  21.1 2.9 fusion.48
  24.8 1.3 collective-permute-start.3
  26.2 2.7 reshape.270
  28.9 2.2 copy.37
  33.0 2.8 fusion.47
  35.9 15.2 %multiply_convert_fusion.2 = (bf16[641,1280]{1,0:T(8,128)(2,1)}, bf16[641,1280]{1,0:T(8,128)(2,1)}) fusion(f32[641]{0:T(1024)S(1)} %fusion.74, f32[641]{0:T(1024)S(1)} %select_multiply_fusion), kind=kLoop, calls=%fused_computation.89 | loop fusion | flops 10666240 | bytes 3287048 | tf_op jit(solution)/shard_map/convert.12
  51.9 9.4 %concatenate.35 = bf16[2,1030,512]{2,1,0:T(8,128)(2,1)S(1)} concatenate(bf16[2,3,512]{2,1,0:T(4,128)(2,1)S(1)} %collective-permute-done, bf16[2,1024,512]{2,1,0:T(8,128)(2,1)} %param.8, bf16[2,3,512]{2,1,0:T(4,128)(2,1)S(1)} %collective-permute-done.1), dimensions={1} | concatenate | bytes 4218880 | tf_op jit(solution)/shard_map/concatenate | solution.py:40
  61.3 2.6 convert_element_type.164
  63.8 4.7 fusion.55
  68.5 3.2 pad_maximum_fusion.1
  71.7 10.2 %copy.40 = bf16[2,1024,4,320]{1,0,3,2:T(2,128)(2,1)} copy(bf16[2,1024,4,320]{1,3,0,2:T(8,128)(2,1)} %pad_maximum_fusion.1) | data formatting | bytes 10485760 | tf_op jit(solution)/shard_map/stack | solution.py:216
  81.9 4.8 copy.45
  86.7 9.7 %fusion.49 = f32[2048,1282]{0,1:T(8,128)} fusion(bf16[2048,1280]{0,1:T(8,128)(2,1)S(1)} %bitcast.122, bf16[641,1280]{1,0:T(8,128)(2,1)S(1)} %copy-done.20, bf16[641,1280]{1,0:T(8,128)(2,1)S(1)} %copy-done.21), kind=kOutput, calls=%fused_computation.122 | convolution fusion | flops 6727936000 | bytes 19026944 | tf_op jit(solution)/shard_map/dot_general | solution.py:104
  96.5 25.9 %all-gather.2.cloned.1.call-done = bf16[216,32,512]{2,1,0:T(8,128)(2,1)} async-done(((bf16[27,32,512]{2,1,0:T(8,128)(2,1)}), bf16[216,32,512]{2,1,0:T(8,128)(2,1)}) %all-gather.2.cloned.1.call-update) | async-done | bytes 7077904 | tf_op jit(solution)/shard_map/all_gather | solution.py:120
  122.3 10.9 %gather_fusion = bf16[137,32,512]{2,1,0:T(8,128)(2,1)} fusion(bf16[216,32,512]{2,1,0:T(8,128)(2,1)} %all-gather.2.cloned.1.call-done, s32[1024]{0:T(1024)S(1)} %pad_clamp_fusion.1), kind=kCustom, calls=%fused_computation | custom fusion | bytes 8978980 | tf_op jit(solution)/shard_map/jit(_take)/gather | solution.py:121
  133.3 4.1 bitcast_select_fusion
  137.5 2.6 broadcast_select_fusion
  140.2 2.4 slice-done
  142.7 6.1 %fusion.88 = (f32[2,1024]{1,0:T(2,128)S(1)}, f32[2,1024,512]{2,1,0:T(8,128)S(1)}) fusion(f32[512]{0:T(512)S(1)} %bitcast.134, f32[2,1030,512]{2,1,0:T(8,128)S(1)} %bitcast.114, f32[2,1024]{1,0:T(2,128)S(1)} %get-tuple-element.69, f32[512]{0:T(512)S(1)} %bitcast.136, f32[2,1024]{1,0:T(2,128)S(1)} %get-tuple-element.70, f32[512]{0:T(512)S(1)} %bitcast.138, ...), kind=kLoop, calls=%fused_computation.211 | loop fusion | flops 22018048 | bytes 33628160 | tf_op jit(solution)/shard_map/jvp()/reduce_sum | solution.py:86
  149.7 2.4 bitcast_subtract_fusion
  152.1 2.5 fusion.60
  154.7 2.3 fusion.89
  157.8 4.0 add_convert_fusion.3
  161.8 31.4 %multiply_convert_fusion = (bf16[2048,1536]{1,0:T(8,128)(2,1)S(1)}, f32[2048,1536]{1,0:T(8,128)}, f32[2048,1536]{1,0:T(8,128)}) fusion(f32[1536]{0:T(1024)S(1)} %reshape.280, bf16[2048,512]{1,0:T(8,128)(2,1)S(1)} %add_convert_fusion.3, bf16[1536,512]{1,0:T(8,128)(2,1)S(1)} %bitcast.123), kind=kOutput, calls=%fused_computation.6 | convolution fusion | flops 3428843520 | bytes 35133440 | tf_op jit(solution)/shard_map/dot_general | solution.py:104
  193.2 5.6 %fusion.86 = (f32[2048]{0:T(1024)S(1)}, f32[2048,512]{1,0:T(8,128)S(1)}, f32[2048,512]{1,0:T(8,128)}) fusion(f32[512]{0:T(512)S(1)} %bitcast.159, f32[512]{0:T(512)S(1)} %bitcast.157, bf16[2,1024,512]{2,1,0:T(8,128)(2,1)S(1)} %copy-done.16, bf16[2048,1536]{1,0:T(8,128)(2,1)S(1)} %get-tuple-element.32, bf16[1536,512]{1,0:T(8,128)(2,1)S(1)} %bitcast.125), kind=kOutput, calls=%fused_computation.210 | convolution fusion | flops 3226466304 | bytes 18362368 | tf_op jit(solution)/shard_map/dot_general | solution.py:104
  198.8 1.9 copy-done.8
  201.6 5.8 %convolution_add_fusion = f32[2048,1282]{0,1:T(8,128)S(1)} fusion(f32[1282]{0:T(1024)S(1)} %slice_convert_fusion.1, bf16[4384,512]{1,0:T(8,128)(2,1)} %copy-done.13, f32[2048,512]{1,0:T(8,128)} %copy-done.8, f32[512]{0:T(512)S(1)} %bitcast.169, f32[512]{0:T(512)S(1)} %bitcast.163, f32[2048]{0:T(1024)S(1)} %fusion.70, f32[2048]{0:T(1024)S(1)} %broadcast_multiply_fusion), kind=kOutput, calls=%fused_computation.22 | convolution fusion | flops 2696417280 | bytes 16040968 | tf_op jit(solution)/shard_map/dot_general | solution.py:104
  207.5 24.2 %add_convert_fusion.1 = (bf16[2048,641]{0,1:T(8,128)(2,1)S(1)}, bf16[2048,641]{0,1:T(8,128)(2,1)S(1)}, bf16[2048,641]{0,1:T(8,128)(2,1)}, bf16[2048,641]{0,1:T(8,128)(2,1)}) fusion(f32[2048,1282]{0,1:T(8,128)} %fusion.49, f32[2048,1282]{0,1:T(8,128)S(1)} %convolution_add_fusion), kind=kLoop, calls=%fused_computation.31 | loop fusion | flops 15753216 | bytes 31506432 | tf_op jit(solution)/shard_map/convert.2
  231.7 1.3 convert_reduce_fusion.1
  233.9 6.2 %multiply_reduce_fusion = (f32[512]{0:T(512)S(1)}, f32[2048]{0:T(1024)S(1)}, f32[512]{0:T(512)S(1)}, f32[2048,512]{1,0:T(8,128)S(1)}) fusion(f32[2048,512]{1,0:T(8,128)S(1)} %copy-done.9, f32[2048]{0:T(1024)S(1)} %fusion.70, f32[2048]{0:T(1024)S(1)} %broadcast_multiply_fusion, f32[512]{0:T(512)S(1)} %bitcast.164, bf16[4384,512]{1,0:T(8,128)(2,1)} %copy-done.13, ...), kind=kOutput, calls=%fused_computation.64 | convolution fusion | flops 2707436544 | bytes 14989312 | tf_op jit(solution)/shard_map/dot_general | solution.py:104
  240.1 4.6 fusion.52
  244.7 2.0 fusion.85
  249.5 3.6 fusion.95
  253.1 16.6 %convert_reduce_fusion = (f32[1536]{0:T(1024)S(1)}, bf16[2048,1536]{1,0:T(8,128)(2,1)}) fusion(f32[2048,1536]{1,0:T(8,128)} %get-tuple-element.33, bf16[2048,512]{1,0:T(8,128)(2,1)} %copy-done.19, bf16[1536,512]{1,0:T(8,128)(2,1)} %bitcast.126, f32[2048,1536]{1,0:T(8,128)} %get-tuple-element.84, f32[1536]{0:T(1024)S(1)} %reshape.280), kind=kOutput, calls=%fused_computation.4 | convolution fusion | flops 3274701312 | bytes 35139584 | tf_op jit(solution)/shard_map/dot_general | solution.py:104
  269.7 6.7 %multiply_reduce_fusion.9 = (f32[2048]{0:T(1024)S(1)}, f32[2048,512]{1,0:T(8,128)S(1)}) fusion(f32[2048,512]{1,0:T(8,128)S(1)} %copy-done.4, f32[2048,512]{1,0:T(8,128)S(1)} %copy-done.6, bf16[2048,1536]{1,0:T(8,128)(2,1)} %get-tuple-element.90, bf16[1536,512]{1,0:T(8,128)(2,1)} %bitcast.124), kind=kOutput, calls=%fused_computation.76 | convolution fusion | flops 3224369152 | bytes 20455424 | tf_op jit(solution)/shard_map/dot_general | solution.py:104
  276.4 5.1 fusion.94
  281.5 2.2 fusion.27
  283.7 1.7 fusion.59
  285.5 5.5 %fusion.84 = (f32[2048]{0:T(1024)S(1)}, f32[2048,512]{1,0:T(8,128)S(1)}) fusion(f32[2048]{0:T(1024)S(1)} %fusion.69, f32[2048]{0:T(1024)S(1)} %copy-done.39, f32[2048,512]{1,0:T(8,128)} %copy-done.7, f32[2048,512]{1,0:T(8,128)} %fusion.60, f32[2048]{0:T(1024)S(1)} %bitcast.132, f32[2,1024,512]{2,1,0:T(8,128)} %copy-done), kind=kLoop, calls=%fused_computation.208 | loop fusion | flops 7337984 | bytes 16809984 | tf_op jit(solution)/shard_map/transpose(jvp())/reduce_sum | solution.py:87
  291.5 3.2 slice-done.2
  294.7 5.3 multiply_reduce_fusion.2
  300.1 27.2 %concatenate.42 = f32[4380,512]{1,0:T(8,128)} concatenate(f32[1536,512]{1,0:T(8,128)} %fusion.94, f32[1536,512]{1,0:T(8,128)S(1)} %fusion.95, f32[1282,512]{1,0:T(8,128)} %fusion.52, f32[1,512]{1,0:T(1,128)S(1)} %bitcast.156, f32[1,512]{1,0:T(1,128)S(1)} %bitcast.155, f32[1,512]{1,0:T(1,128)S(1)} %bitcast.154, f32[1,512]{1,0:T(1,128)S(1)} %bitcast.153, f32[1,512]{1,0:T(1,128)S(1)} %bitcast.152, ...), dimensions={0} | concatenate | bytes 17940480 | tf_op jit(solution)/shard_map/concatenate | solution.py:293
  327.2 8.1 %pad.35 = f32[4384,512]{1,0:T(8,128)} pad(f32[4380,512]{1,0:T(8,128)} %concatenate.42, f32[]{:T(128)} %constant.72.clone.1), padding=0_4x0_0 | pad | bytes 17948676 | tf_op jit(solution)/shard_map/jit(_pad)/pad | solution.py:296
  335.3 1.7 copy-done.15
  337.1 13.9 %fusion.6 = f32[2048,1280]{0,1:T(8,128)} fusion(bf16[2048,641]{0,1:T(8,128)(2,1)} %get-tuple-element.41, bf16[2048,641]{0,1:T(8,128)(2,1)S(1)} %copy-done.15, bf16[641,1280]{1,0:T(8,128)(2,1)} %get-tuple-element.91, bf16[641,1280]{1,0:T(8,128)(2,1)} %get-tuple-element.92), kind=kOutput, calls=%fused_computation.34 | convolution fusion | flops 6738438144 | bytes 19018752 | tf_op jit(solution)/shard_map/dot_general | solution.py:104
  350.9 14.4 %reshape.268 = f32[2,1024,4,320]{1,0,3,2:T(2,128)} reshape(f32[2048,1280]{0,1:T(8,128)} %fusion.6) | data formatting | bytes 20971520 | tf_op jit(solution)/shard_map/reshape | solution.py:189
  365.4 8.5 %copy_multiply_fusion = f32[2,1024,4,320]{1,3,0,2:T(8,128)S(1)} fusion(f32[2,1024,4,320]{1,0,3,2:T(2,128)} %reshape.268, f32[4,320]{1,0:T(4,128)S(1)} %copy-done.52), kind=kLoop, calls=%fused_computation.21 | loop fusion | flops 2621440 | bytes 20976640 | tf_op jit(solution)/shard_map/mul | solution.py:189
  374.2 1.8 fusion.46
  376.4 1.5 collective-permute-start.2
  377.9 2.3 pad_add_fusion
  382.3 4.4 collective-permute-start.5
  386.8 2.4 fusion.43
  389.2 2.6 copy.36
  391.9 4.1 reshape.269
  396.1 20.3 %fusion.13 = f32[2,1024,512]{2,1,0:T(8,128)} fusion(f32[2,3,512]{2,1,0:T(4,128)S(1)} %collective-permute-done.5, f32[2,3,512]{2,1,0:T(4,128)S(1)} %collective-permute-done.4, f32[2,1024,512]{2,1,0:T(8,128)} %bitcast.119, f32[2,1024,512]{2,1,0:T(8,128)} %bitcast.118, f32[512]{0:T(512)S(1)} %bitcast.135, f32[2,1024]{1,0:T(2,128)S(1)} %copy-done.31, ...), kind=kLoop, calls=%fused_computation.46 | loop fusion | flops 27262976 | bytes 12670976 | tf_op jit(solution)/shard_map/add | solution.py:279
  416.3 103.8 %all-reduce.10.cloned.1.call-done = f32[137,32,512]{2,1,0:T(8,128)} async-done(((f32[137,32,512]{2,1,0:T(8,128)}), f32[137,32,512]{2,1,0:T(8,128)}) %all-reduce.10.cloned.1.call-update) | async-done | bytes 8978448 | tf_op jit(solution)/shard_map/psum | solution.py:298
  520.2 9.1 %concatenate.43 = f32[138,32,512]{2,1,0:T(8,128)} pad(f32[137,32,512]{2,1,0:T(8,128)} %all-reduce.10.cloned.1.call-done, f32[]{:T(128)} %constant.72.clone.1), padding=0_1x0_0x0_0 | pad | bytes 18022404 | tf_op jit(solution)/shard_map/concatenate | solution.py:299
  529.3 4.5 gather_fusion.1
  533.8 5.5 %multiply_subtract_fusion = (f32[27,32,512]{2,1,0:T(8,128)}, f32[27,32,512]{2,1,0:T(8,128)}, f32[27,32,512]{2,1,0:T(8,128)}) fusion(f32[27,32,512]{2,1,0:T(8,128)S(1)} %copy-done.12, f32[27,32,512]{2,1,0:T(8,128)S(1)} %gather_fusion.1, pred[27]{0:T(512)(128)(4,1)S(1)} %copy-done.68, f32[27,32,512]{2,1,0:T(8,128)} %param.13, f32[27,32,512]{2,1,0:T(8,128)} %param.14), kind=kLoop, calls=%fused_computation.127 | loop fusion | flops 7077888 | bytes 12386331 | tf_op jit(solution)/shard_map/sub | solution.py:306
  (220 shorter events, 16.0 us)
Async XLA Ops:
  7.2 115.2 %all-gather.2.cloned.1.call-start = ((), (), s32[]{:S(2)}) async-start(), calls=%async_computation | async-start | bytes 7962624 | tf_op jit(solution)/shard_map/all_gather | solution.py:120
  9.8 510.4 %all-reduce.10.cloned.1.call-start = ((), (), s32[]{:S(2)}) async-start(), calls=%async_computation.1 | async-start | bytes 17956864 | tf_op jit(solution)/shard_map/psum | solution.py:298
  10.6 41.3 %collective-permute-start = (bf16[2,3,512]{2,1,0:T(4,128)(2,1)S(1)}, bf16[2,3,512]{2,1,0:T(4,128)(2,1)S(1)}, u32[]{:S(2)}, u32[]{:S(2)}) collective-permute-start(bf16[2,3,512]{2,1,0:T(4,128)(2,1)S(1)} %get-tuple-element.55), channel_id=1, source_target_pairs={{0,1},{1,2},{2,3},{4,5},{5,6},{6,7},{8,9},{9,10},{10,11},{12,13},{... | collective-permute-start | bytes 18440 | tf_op jit(solution)/shard_map/ppermute | solution.py:36
  12.9 38.9 %collective-permute-start.1 = (bf16[2,3,512]{2,1,0:T(4,128)(2,1)S(1)}, bf16[2,3,512]{2,1,0:T(4,128)(2,1)S(1)}, u32[]{:S(2)}, u32[]{:S(2)}) collective-permute-start(bf16[2,3,512]{2,1,0:T(4,128)(2,1)S(1)} %get-tuple-element.54), channel_id=1, source_target_pairs={{1,0},{2,1},{3,2},{5,4},{6,5},{7,6},{9,8},{10,9},{11,10},{13,12},{... | collective-permute-start | bytes 18440 | tf_op jit(solution)/shard_map/ppermute | solution.py:39
  20.9 12.1 %copy-start.44 = (f32[320]{0:T(512)}, f32[320]{0:T(512)S(1)}, u32[]{:S(2)}) copy-start(f32[320]{0:T(512)S(1)} %get-tuple-element.75) | copy-start | bytes 3844
  20.9 12.1 %copy-start.46 = (f32[320]{0:T(512)}, f32[320]{0:T(512)S(1)}, u32[]{:S(2)}) copy-start(f32[320]{0:T(512)S(1)} %get-tuple-element.76) | copy-start | bytes 3844
  20.9 12.1 %copy-start.48 = (f32[320]{0:T(512)}, f32[320]{0:T(512)S(1)}, u32[]{:S(2)}) copy-start(f32[320]{0:T(512)S(1)} %get-tuple-element.77) | copy-start | bytes 3844
  20.9 12.1 %copy-start.50 = (f32[320]{0:T(512)}, f32[320]{0:T(512)S(1)}, u32[]{:S(2)}) copy-start(f32[320]{0:T(512)S(1)} %get-tuple-element.78) | copy-start | bytes 3844
  21.1 119.1 %copy-start.24 = (f32[2,1024]{1,0:T(2,128)}, f32[2,1024]{1,0:T(2,128)S(1)}, u32[]{:S(2)}) copy-start(f32[2,1024]{1,0:T(2,128)S(1)} %get-tuple-element.68) | copy-start | bytes 24580
  21.1 119.1 %copy-start.26 = (f32[2,1024]{1,0:T(2,128)}, f32[2,1024]{1,0:T(2,128)S(1)}, u32[]{:S(2)}) copy-start(f32[2,1024]{1,0:T(2,128)S(1)} %get-tuple-element.72) | copy-start | bytes 24580
  21.1 119.1 %copy-start.28 = (f32[2,1024]{1,0:T(2,128)}, f32[2,1024]{1,0:T(2,128)S(1)}, u32[]{:S(2)}) copy-start(f32[2,1024]{1,0:T(2,128)S(1)} %get-tuple-element.73) | copy-start | bytes 24580
  21.1 119.1 %copy-start.30 = (f32[2,1024]{1,0:T(2,128)}, f32[2,1024]{1,0:T(2,128)S(1)}, u32[]{:S(2)}) copy-start(f32[2,1024]{1,0:T(2,128)S(1)} %get-tuple-element.69) | copy-start | bytes 24580
  21.1 119.1 %copy-start.32 = (f32[2,1024]{1,0:T(2,128)}, f32[2,1024]{1,0:T(2,128)S(1)}, u32[]{:S(2)}) copy-start(f32[2,1024]{1,0:T(2,128)S(1)} %get-tuple-element.70) | copy-start | bytes 24580
  21.1 119.1 %copy-start.34 = (f32[2,1024]{1,0:T(2,128)}, f32[2,1024]{1,0:T(2,128)S(1)}, u32[]{:S(2)}) copy-start(f32[2,1024]{1,0:T(2,128)S(1)} %get-tuple-element.71) | copy-start | bytes 24580
  24.8 39.0 %collective-permute-start.3 = (f32[2,3,320]{1,2,0:T(8,128)}, f32[2,3,320]{1,2,0:T(8,128)}, u32[]{:S(2)}, u32[]{:S(2)}) collective-permute-start(f32[2,3,320]{1,2,0:T(8,128)} %slice.387), channel_id=1, source_target_pairs={{1,0},{2,1},{3,2},{5,4},{6,5},{7,6},{9,8},{10,9},{11,10},{13,12},{... | collective-permute-start | bytes 23048 | tf_op jit(solution)/shard_map/ppermute | solution.py:47
  26.2 4.9 copy-start.67
  26.2 6.7 %copy-start.69 = (s32[2,4]{1,0:T(2,128)S(1)}, s32[2,4]{1,0:T(2,128)}, u32[]{:S(2)}) copy-start(s32[2,4]{1,0:T(2,128)} %param.10) | copy-start | bytes 100
  51.8 105.1 %copy-start.36 = (s32[1,8,2,128]{3,1,2,0:T(8,128)}, s32[1,8,2,128]{3,1,2,0:T(8,128)S(1)}, u32[]{:S(2)}) copy-start(s32[1,8,2,128]{3,1,2,0:T(8,128)S(1)} %copy.53) | copy-start | bytes 24580
  81.9 4.8 copy-start.20
  81.9 4.8 copy-start.21
  133.3 4.2 copy-start.1
  137.4 14.7 %copy-start.13 = (bf16[4384,512]{1,0:T(8,128)(2,1)}, bf16[4384,512]{1,0:T(8,128)(2,1)S(1)}, u32[]{:S(2)}) copy-start(bf16[4384,512]{1,0:T(8,128)(2,1)S(1)} %bitcast_select_fusion) | copy-start | bytes 13467652
  137.4 5.3 slice-start
  137.5 5.2 slice-start.1
  140.1 8.7 %copy-start.53 = (f32[1,512]{1,0:T(1,128)}, f32[1,512]{1,0:T(1,128)S(1)}, u32[]{:S(2)}) copy-start(f32[1,512]{1,0:T(1,128)S(1)} %get-tuple-element.59) | copy-start | bytes 6148
  140.1 8.7 %copy-start.55 = (f32[1,512]{1,0:T(1,128)}, f32[1,512]{1,0:T(1,128)S(1)}, u32[]{:S(2)}) copy-start(f32[1,512]{1,0:T(1,128)S(1)} %get-tuple-element.60) | copy-start | bytes 6148
  140.1 8.7 %copy-start.57 = (f32[1,512]{1,0:T(1,128)}, f32[1,512]{1,0:T(1,128)S(1)}, u32[]{:S(2)}) copy-start(f32[1,512]{1,0:T(1,128)S(1)} %get-tuple-element.61) | copy-start | bytes 6148
  140.1 8.7 %copy-start.59 = (f32[1,512]{1,0:T(1,128)}, f32[1,512]{1,0:T(1,128)S(1)}, u32[]{:S(2)}) copy-start(f32[1,512]{1,0:T(1,128)S(1)} %get-tuple-element.62) | copy-start | bytes 6148
  140.2 8.7 %copy-start.61 = (f32[1,512]{1,0:T(1,128)}, f32[1,512]{1,0:T(1,128)S(1)}, u32[]{:S(2)}) copy-start(f32[1,512]{1,0:T(1,128)S(1)} %get-tuple-element.63) | copy-start | bytes 6148
  140.2 8.7 %copy-start.63 = (f32[1,512]{1,0:T(1,128)}, f32[1,512]{1,0:T(1,128)S(1)}, u32[]{:S(2)}) copy-start(f32[1,512]{1,0:T(1,128)S(1)} %get-tuple-element.64) | copy-start | bytes 6148
  140.2 8.7 %copy-start.65 = (f32[1,512]{1,0:T(1,128)}, f32[1,512]{1,0:T(1,128)S(1)}, u32[]{:S(2)}) copy-start(f32[1,512]{1,0:T(1,128)S(1)} %get-tuple-element.65) | copy-start | bytes 6148
  149.7 7.2 %copy-start.38 = (f32[2048]{0:T(1024)}, f32[2048]{0:T(1024)S(1)}, u32[]{:S(2)}) copy-start(f32[2048]{0:T(1024)S(1)} %bitcast_rsqrt_fusion) | copy-start | bytes 24580
  157.8 4.0 copy-start.22
  157.8 35.4 %copy-start.23 = (bf16[48,32,512]{2,1,0:T(8,128)(2,1)}, bf16[48,32,512]{2,1,0:T(8,128)(2,1)S(1)}, u32[]{:S(2)}) copy-start(bf16[48,32,512]{2,1,0:T(8,128)(2,1)S(1)} %get-tuple-element.45) | copy-start | bytes 4718596
  161.8 31.4 %copy-start.17 = (bf16[2048,512]{1,0:T(8,128)(2,1)}, bf16[2048,512]{1,0:T(8,128)(2,1)S(1)}, u32[]{:S(2)}) copy-start(bf16[2048,512]{1,0:T(8,128)(2,1)S(1)} %add_convert_fusion.3) | copy-start | bytes 6291460
  161.8 31.4 %copy-start.16 = (bf16[2,1024,512]{2,1,0:T(8,128)(2,1)S(1)}, bf16[2,1024,512]{2,1,0:T(8,128)(2,1)}, u32[]{:S(2)}) copy-start(bf16[2,1024,512]{2,1,0:T(8,128)(2,1)} %param.8) | copy-start | bytes 6291460
  193.2 5.6 %copy-start.71 = (bf16[2048,1536]{1,0:T(8,128)(2,1)}, bf16[2048,1536]{1,0:T(8,128)(2,1)S(1)}, u32[]{:S(2)}) copy-start(bf16[2048,1536]{1,0:T(8,128)(2,1)S(1)} %get-tuple-element.32) | copy-start | bytes 18874372
  247.5 5.6 %copy-start.5 = (f32[2048,512]{1,0:T(8,128)}, f32[2048,512]{1,0:T(8,128)S(1)}, u32[]{:S(2)}) copy-start(f32[2048,512]{1,0:T(8,128)S(1)} %get-tuple-element.21) | copy-start | bytes 12582916
  248.2 4.9 copy-start.19
  253.1 16.6 %copy-start.4 = (f32[2048,512]{1,0:T(8,128)S(1)}, f32[2048,512]{1,0:T(8,128)}, u32[]{:S(2)}) copy-start(f32[2048,512]{1,0:T(8,128)} %bitcast_subtract_fusion) | copy-start | bytes 12582916
  253.1 16.6 %copy-start.6 = (f32[2048,512]{1,0:T(8,128)S(1)}, f32[2048,512]{1,0:T(8,128)}, u32[]{:S(2)}) copy-start(f32[2048,512]{1,0:T(8,128)} %fusion.60) | copy-start | bytes 12582916
  269.7 6.7 %copy-start.18 = (bf16[2048,512]{1,0:T(8,128)(2,1)S(1)}, bf16[2048,512]{1,0:T(8,128)(2,1)}, u32[]{:S(2)}) copy-start(bf16[2048,512]{1,0:T(8,128)(2,1)} %copy-done.17) | copy-start | bytes 6291460
  269.7 6.7 %copy-start.70 = (bf16[2048,1536]{1,0:T(8,128)(2,1)S(1)}, bf16[2048,1536]{1,0:T(8,128)(2,1)}, u32[]{:S(2)}) copy-start(bf16[2048,1536]{1,0:T(8,128)(2,1)} %get-tuple-element.90) | copy-start | bytes 18874372
  276.4 7.3 %copy-start.7 = (f32[2048,512]{1,0:T(8,128)}, f32[2048,512]{1,0:T(8,128)S(1)}, u32[]{:S(2)}) copy-start(f32[2048,512]{1,0:T(8,128)S(1)} %get-tuple-element.88) | copy-start | bytes 12582916
  276.4 5.1 copy-start.37
  276.4 5.1 copy-start.39
  291.5 8.6 %copy-start.2 = (f32[2048,512]{1,0:T(8,128)}, f32[2048,512]{1,0:T(8,128)S(1)}, u32[]{:S(2)}) copy-start(f32[2048,512]{1,0:T(8,128)S(1)} %get-tuple-element.25) | copy-start | bytes 12582916
  350.9 14.4 %copy-start.52 = (f32[4,320]{1,0:T(4,128)S(1)}, f32[4,320]{1,0:T(4,128)}, u32[]{:S(2)}) copy-start(f32[4,320]{1,0:T(4,128)} %multiply_subtract_fusion.2) | copy-start | bytes 15364
  376.4 10.4 %copy-start.45 = (f32[320]{0:T(512)S(1)}, f32[320]{0:T(512)}, u32[]{:S(2)}) copy-start(f32[320]{0:T(512)} %copy-done.44) | copy-start | bytes 3844
  376.4 10.4 %copy-start.47 = (f32[320]{0:T(512)S(1)}, f32[320]{0:T(512)}, u32[]{:S(2)}) copy-start(f32[320]{0:T(512)} %copy-done.46) | copy-start | bytes 3844
  376.4 10.4 %copy-start.49 = (f32[320]{0:T(512)S(1)}, f32[320]{0:T(512)}, u32[]{:S(2)}) copy-start(f32[320]{0:T(512)} %copy-done.48) | copy-start | bytes 3844
  376.4 10.4 %copy-start.51 = (f32[320]{0:T(512)S(1)}, f32[320]{0:T(512)}, u32[]{:S(2)}) copy-start(f32[320]{0:T(512)} %copy-done.50) | copy-start | bytes 3844
  376.4 10.3 %collective-permute-start.2 = (f32[2,3,320]{1,2,0:T(8,128)S(1)}, f32[2,3,320]{1,2,0:T(8,128)S(1)}, u32[]{:S(2)}, u32[]{:S(2)}) collective-permute-start(f32[2,3,320]{1,2,0:T(8,128)S(1)} %pad_add_fusion.1), channel_id=1, source_target_pairs={{0,1},{1,2},{2,3},{4,5},{5,6},{6,7},{8,9},{9,10},{10,11},{12,13},{... | collective-permute-start | bytes 23048 | tf_op jit(solution)/shard_map/ppermute | solution.py:47
  381.1 14.9 %collective-permute-start.4 = (f32[2,3,512]{2,1,0:T(4,128)S(1)}, f32[2,3,512]{2,1,0:T(4,128)S(1)}, u32[]{:S(2)}, u32[]{:S(2)}) collective-permute-start(f32[2,3,512]{2,1,0:T(4,128)S(1)} %get-tuple-element.49), channel_id=1, source_target_pairs={{1,0},{2,1},{3,2},{5,4},{6,5},{7,6},{9,8},{10,9},{11,10},{13,12},{... | collective-permute-start | bytes 36872 | tf_op jit(solution)/shard_map/ppermute | solution.py:39
  382.3 13.6 %collective-permute-start.5 = (f32[2,3,512]{2,1,0:T(4,128)S(1)}, f32[2,3,512]{2,1,0:T(4,128)S(1)}, u32[]{:S(2)}, u32[]{:S(2)}) collective-permute-start(f32[2,3,512]{2,1,0:T(4,128)S(1)} %get-tuple-element.50), channel_id=1, source_target_pairs={{0,1},{1,2},{2,3},{4,5},{5,6},{6,7},{8,9},{9,10},{10,11},{12,13},{... | collective-permute-start | bytes 36872 | tf_op jit(solution)/shard_map/ppermute | solution.py:36
  391.9 4.1 copy-start.54
  391.9 4.1 copy-start.56
  391.9 4.1 copy-start.58
  391.9 4.1 copy-start.60
  391.9 4.1 copy-start.62
  391.9 4.1 copy-start.64
  391.9 4.1 copy-start.66
  416.3 117.4 %copy-start.68 = (pred[27]{0:T(512)(128)(4,1)S(1)}, pred[27]{0:T(512)(128)(4,1)}, u32[]{:S(2)}) copy-start(pred[27]{0:T(512)(128)(4,1)} %get-tuple-element.18) | copy-start | bytes 85
  529.3 4.5 copy-start.12
  (22 other events, 63.2 us)
Sparse Core Ops, SparseCore 0:
  10.8 111.5 all-gather.1
  335.5 184.6 all-reduce.9
where the time goes:
time: 556 us; the launch traced here: 546 us
  other arithmetic  136 us (24%)
  local copies, waits for them, and re-layouts  133 us (24%)
  waiting for transfers between devices  130 us (23%)
  matrix products  119 us (21%)
  between operations  15.7 us (3%)
  starting transfers between devices  12.2 us (2%)
    dot_general x11, matrix products, contract(): lax.dot_general(left_side, right_side, (((left_dim,), (right_dim,)), ((),...  109 us
    psum x1, waiting for transfers between devices, local(): summed = lax.psum(grad_buckets, ('rows', 'seq'))  104 us
    another operation x3, other arithmetic  42.2 us
    concatenate x1, local copies, waits for them, and re-layouts, local(): jnp.concatenate([grad_w_in, grad_w_out, grad_w_head, vec_grads, in_rows,...  27.2 us
    all_gather x1, waiting for transfers between devices, local(): lax.all_gather(master.astype(jnp.bfloat16), 'rows', axis=0, tiled=True)  25.9 us
    add x1, other arithmetic, local(): input_grad + conv_weight[tap_index] * keep * halo_grad[:, begin:begin + f...  20.3 us
    unnamed x159, local copies, waits for them, and re-layouts  17.5 us
    reshape x1, local copies, waits for them, and re-layouts, local(): signal.reshape(rows_here, frames_here, lap_count, HOP)  14.4 us
  transfers between devices with their start and end apart: 8, of which 2 were waited for; matrix products, arithmetic and copies ran while one was open for 28% of the time, Pallas kernels for 0%

commit v1 on v0

--- a/solution.py
+++ b/solution.py
@@ -28,6 +28,29 @@
 ADAM_EPS = 1e-08
 
 
+def measure_bands_now(matrix):
+    s_next, block_next, val = (lax.axis_size("rows"), lax.axis_index("rows"), matrix.shape[0])
+    buffer = [(dev_j, (dev_j + 1) % s_next) for dev_j in range(s_next)]
+    vec_out = jnp.zeros((*matrix.shape[:0], s_next * val, *matrix.shape[1:]), matrix.dtype)
+    vec_out = lax.dynamic_update_slice_in_dim(vec_out, matrix, block_next * val, axis=0)
+    w_next = r1 = matrix
+    trail = [(dev_j, (dev_j - 1) % s_next) for dev_j in range(s_next)]
+    carry_out = s_next // 2
+    w = 1
+    while w < carry_out + 1:
+        w_next = lax.ppermute(w_next, "rows", buffer)
+        vec_out = lax.dynamic_update_slice_in_dim(
+            vec_out, w_next, (block_next - w) % s_next * val, axis=0
+        )
+        if w < s_next - carry_out:
+            r1 = lax.ppermute(r1, "rows", trail)
+            vec_out = lax.dynamic_update_slice_in_dim(
+                vec_out, r1, (block_next + w) % s_next * val, axis=0
+            )
+        w += 1
+    return vec_out
+
+
 def padded(block, sides, width):
     for axis, dim in sides:
         count = lax.axis_size(axis)
@@ -117,7 +140,7 @@
     rim_width = (KW - 1) // 2
     margin = max(rim_width, lap_count - 1)
     bucket_place, source = slot_maps(owner_list, lax.axis_size("rows"), slot_count)
-    gathered = lax.all_gather(master.astype(jnp.bfloat16), "rows", axis=0, tiled=True)
+    gathered = measure_bands_now(master.astype(jnp.bfloat16))
     buckets = jnp.take(gathered, bucket_place, axis=0)
     weight_table = buckets.reshape(-1, channels)[:PR]
     w_in = weight_table[:FF]

time: 556 us -> 597 us (1.074)
  waiting for transfers between devices: 130 us -> 149 us
  starting transfers between devices: 12.2 us -> 26.4 us
  local copies, waits for them, and re-layouts: 133 us -> 143 us
    ppermute x0 -> x7, waiting for transfers between devices: none -> 41.7 us  [the longest x3 30.6 us: measure_bands_now(): r1 = lax.ppermute(r1, 'rows', trail)]
    all_gather x1 -> x0, waiting for transfers between devices: 25.9 us -> none  [local(): lax.all_gather(master.astype(jnp.bfloat16), 'rows', axis=0, tiled=True)]
    ppermute x0 -> x7, starting transfers between devices: none -> 14.8 us  [the longest x3 8.78 us: measure_bands_now(): r1 = lax.ppermute(r1, 'rows', trail)]
    dynamic_update_slice x0 -> x7, local copies, waits for them, and re-layouts: none -> 10.5 us  [the longest x4 6.35 us: measure_bands_now(): lax.dynamic_update_slice_in_dim(vec_out, w_next, (block_next - w) % s_nex...]
    unnamed x159 -> x163, local copies, waits for them, and re-layouts: 17.5 us -> 15.5 us
  transfers between devices with their start and end apart: 8 -> 14, of which waited for: 2 -> 4; matrix products, arithmetic and copies ran while one was open for 28% -> 28% of each run, Pallas kernels for 0% -> 0%
where the time goes in v1:
time: 597 us; the launch traced here: 589 us
  waiting for transfers between devices  149 us (25%)
  local copies, waits for them, and re-layouts  143 us (24%)
  other arithmetic  134 us (22%)
  matrix products  120 us (20%)
  starting transfers between devices  26.4 us (4%)
  between operations  16 us (3%)
    dot_general x11, matrix products, contract(): lax.dot_general(left_side, right_side, (((left_dim,), (right_dim,)), ((),...  108 us
    psum x1, waiting for transfers between devices, local(): summed = lax.psum(grad_buckets, ('rows', 'seq'))  108 us
    another operation x3, other arithmetic  42.4 us
    ppermute x3, waiting for transfers between devices, measure_bands_now(): r1 = lax.ppermute(r1, 'rows', trail)  30.6 us
    concatenate x1, local copies, waits for them, and re-layouts, local(): jnp.concatenate([grad_w_in, grad_w_out, grad_w_head, vec_grads, in_rows,...  27.2 us
    add x1, other arithmetic, local(): input_grad + conv_weight[tap_index] * keep * halo_grad[:, begin:begin + f...  20.7 us
    unnamed x163, local copies, waits for them, and re-layouts  15.5 us
    reshape x1, local copies, waits for them, and re-layouts, local(): signal.reshape(rows_here, frames_here, lap_count, HOP)  14.4 us
  transfers between devices with their start and end apart: 14, of which 4 were waited for; matrix products, arithmetic and copies ran while one was open for 28% of the time, Pallas kernels for 0%

profile of v1, /device:TPU:0, one launch (start us, length us, event | category | flops | bytes accessed | tf_op | source)
XLA Modules:
  0.0 588.6 jit_solution(11173948216280326282)
XLA Ops:
  7.2 3.8 broadcast_in_dim.56
  12.5 2.9 collective-permute-start
  15.4 3.0 collective-permute-start.1
  23.2 2.7 reshape.271
  25.9 2.2 copy.33
  28.1 2.7 fusion.48
  34.5 2.7 reshape.270
  37.2 2.2 copy.31
  39.6 2.9 fusion.47
  42.4 11.1 %collective-permute-done = bf16[27,32,512]{2,1,0:T(8,128)(2,1)} collective-permute-done((bf16[27,32,512]{2,1,0:T(8,128)(2,1)}, bf16[27,32,512]{2,1,0:T(8,128)(2,1)}, u32[]{:S(2)}, u32[]{:S(2)}) %collective-permute-start) | collective-permute-done | bytes 884768 | tf_op jit(solution)/shard_map/ppermute | solution.py:41
  53.6 2.5 collective-permute-start.2
  57.5 15.2 %multiply_convert_fusion.2 = (bf16[641,1280]{1,0:T(8,128)(2,1)}, bf16[641,1280]{1,0:T(8,128)(2,1)}) fusion(f32[641]{0:T(1024)S(1)} %fusion.74, f32[641]{0:T(1024)S(1)} %select_multiply_fusion), kind=kLoop, calls=%fused_computation.89 | loop fusion | flops 10666240 | bytes 3287048 | tf_op jit(solution)/shard_map/convert.12
  73.5 9.3 %concatenate.35 = bf16[2,1030,512]{2,1,0:T(8,128)(2,1)S(1)} concatenate(bf16[2,3,512]{2,1,0:T(4,128)(2,1)S(1)} %collective-permute-done.7, bf16[2,1024,512]{2,1,0:T(8,128)(2,1)} %param.8, bf16[2,3,512]{2,1,0:T(4,128)(2,1)S(1)} %collective-permute-done.8), dimensions={1} | concatenate | bytes 4218880 | tf_op jit(solution)/shard_map/concatenate | solution.py:63
  82.9 2.6 convert_element_type.164
  85.5 3.0 collective-permute-start.3
  88.7 4.7 fusion.55
  93.4 3.0 pad_maximum_fusion.1
  96.4 10.2 %copy.34 = bf16[2,1024,4,320]{1,0,3,2:T(2,128)(2,1)} copy(bf16[2,1024,4,320]{1,3,0,2:T(8,128)(2,1)} %pad_maximum_fusion.1) | data formatting | bytes 10485760 | tf_op jit(solution)/shard_map/stack | solution.py:239
  106.6 4.8 copy.39
  111.4 13.5 %collective-permute-done.3 = bf16[27,32,512]{2,1,0:T(8,128)(2,1)S(1)} collective-permute-done((bf16[27,32,512]{2,1,0:T(8,128)(2,1)}, bf16[27,32,512]{2,1,0:T(8,128)(2,1)S(1)}, u32[]{:S(2)}, u32[]{:S(2)}) %collective-permute-start.3) | collective-permute-done | bytes 884768 | tf_op jit(solution)/shard_map/ppermute | solution.py:46
  124.9 2.7 collective-permute-start.5
  128.0 9.6 %fusion.49 = f32[2048,1282]{0,1:T(8,128)} fusion(bf16[2048,1280]{0,1:T(8,128)(2,1)S(1)} %bitcast.122, bf16[641,1280]{1,0:T(8,128)(2,1)S(1)} %copy-done.20, bf16[641,1280]{1,0:T(8,128)(2,1)S(1)} %copy-done.21), kind=kOutput, calls=%fused_computation.122 | convolution fusion | flops 6727936000 | bytes 19026944 | tf_op jit(solution)/shard_map/dot_general | solution.py:127
  137.5 2.2 constant_dynamic-update-slice_fusion.6
  139.7 2.2 constant_dynamic-update-slice_fusion.5
  141.9 2.2 constant_dynamic-update-slice_fusion.4
  146.1 17.1 %collective-permute-done.5 = bf16[27,32,512]{2,1,0:T(8,128)(2,1)S(1)} collective-permute-done((bf16[27,32,512]{2,1,0:T(8,128)(2,1)S(1)}, bf16[27,32,512]{2,1,0:T(8,128)(2,1)S(1)}, u32[]{:S(2)}, u32[]{:S(2)}) %collective-permute-start.5) | collective-permute-done | bytes 884768 | tf_op jit(solution)/shard_map/ppermute | solution.py:46
  165.1 10.5 %gather_fusion = bf16[137,32,512]{2,1,0:T(8,128)(2,1)} fusion(bf16[216,32,512]{2,1,0:T(8,128)(2,1)} %constant_dynamic-update-slice_fusion, s32[1024]{0:T(1024)S(1)} %pad_clamp_fusion.1), kind=kCustom, calls=%fused_computation | custom fusion | bytes 8978980 | tf_op jit(solution)/shard_map/jit(_take)/gather | solution.py:144
  175.7 2.9 broadcast_select_fusion
  179.3 2.3 bitcast_select_fusion
  181.8 6.1 %fusion.88 = (f32[2,1024]{1,0:T(2,128)S(1)}, f32[2,1024,512]{2,1,0:T(8,128)S(1)}) fusion(f32[512]{0:T(512)S(1)} %bitcast.134, f32[2,1030,512]{2,1,0:T(8,128)S(1)} %bitcast.114, f32[2,1024]{1,0:T(2,128)S(1)} %get-tuple-element.71, f32[512]{0:T(512)S(1)} %bitcast.136, f32[2,1024]{1,0:T(2,128)S(1)} %get-tuple-element.72, f32[512]{0:T(512)S(1)} %bitcast.138, ...), kind=kLoop, calls=%fused_computation.219 | loop fusion | flops 22018048 | bytes 33628160 | tf_op jit(solution)/shard_map/jvp()/reduce_sum | solution.py:109
  189.9 2.3 bitcast_subtract_fusion
  192.2 2.5 fusion.60
  195.0 5.1 add_convert_fusion.3
  200.1 31.6 %multiply_convert_fusion = (bf16[2048,1536]{1,0:T(8,128)(2,1)S(1)}, f32[2048,1536]{1,0:T(8,128)}, f32[2048,1536]{1,0:T(8,128)}) fusion(f32[1536]{0:T(1024)S(1)} %reshape.280, bf16[2048,512]{1,0:T(8,128)(2,1)S(1)} %add_convert_fusion.3, bf16[1536,512]{1,0:T(8,128)(2,1)S(1)} %bitcast.123), kind=kOutput, calls=%fused_computation.6 | convolution fusion | flops 3428843520 | bytes 35133440 | tf_op jit(solution)/shard_map/dot_general | solution.py:127
  231.8 5.4 fusion.86
  237.2 2.0 copy-done.7
  240.0 5.8 convolution_add_fusion
  245.9 24.4 %add_convert_fusion.1 = (bf16[2048,641]{0,1:T(8,128)(2,1)S(1)}, bf16[2048,641]{0,1:T(8,128)(2,1)S(1)}, bf16[2048,641]{0,1:T(8,128)(2,1)}, bf16[2048,641]{0,1:T(8,128)(2,1)}) fusion(f32[2048,1282]{0,1:T(8,128)} %fusion.49, f32[2048,1282]{0,1:T(8,128)S(1)} %convolution_add_fusion), kind=kLoop, calls=%fused_computation.31 | loop fusion | flops 15753216 | bytes 31506432 | tf_op jit(solution)/shard_map/convert.2
  272.5 6.2 %multiply_reduce_fusion = (f32[512]{0:T(512)S(1)}, f32[2048]{0:T(1024)S(1)}, f32[512]{0:T(512)S(1)}, f32[2048,512]{1,0:T(8,128)S(1)}) fusion(f32[2048,512]{1,0:T(8,128)S(1)} %copy-done.8, f32[2048]{0:T(1024)S(1)} %fusion.70, f32[2048]{0:T(1024)S(1)} %broadcast_multiply_fusion, f32[512]{0:T(512)S(1)} %bitcast.164, bf16[4384,512]{1,0:T(8,128)(2,1)} %copy-done.13, ...), kind=kOutput, calls=%fused_computation.64 | convolution fusion | flops 2707436544 | bytes 14989312 | tf_op jit(solution)/shard_map/dot_general | solution.py:127
  278.7 4.6 fusion.52
  283.3 2.2 fusion.85
  287.9 3.6 fusion.95
  291.5 16.5 %convert_reduce_fusion = (f32[1536]{0:T(1024)S(1)}, bf16[2048,1536]{1,0:T(8,128)(2,1)}) fusion(f32[2048,1536]{1,0:T(8,128)} %get-tuple-element.33, bf16[2048,512]{1,0:T(8,128)(2,1)} %copy-done.19, bf16[1536,512]{1,0:T(8,128)(2,1)} %bitcast.126, f32[2048,1536]{1,0:T(8,128)} %get-tuple-element.86, f32[1536]{0:T(1024)S(1)} %reshape.280), kind=kOutput, calls=%fused_computation.4 | convolution fusion | flops 3274701312 | bytes 35139584 | tf_op jit(solution)/shard_map/dot_general | solution.py:127
  308.0 6.4 %multiply_reduce_fusion.9 = (f32[2048]{0:T(1024)S(1)}, f32[2048,512]{1,0:T(8,128)S(1)}) fusion(f32[2048,512]{1,0:T(8,128)S(1)} %copy-done.3, f32[2048,512]{1,0:T(8,128)S(1)} %copy-done.5, bf16[2048,1536]{1,0:T(8,128)(2,1)} %get-tuple-element.92, bf16[1536,512]{1,0:T(8,128)(2,1)} %bitcast.124), kind=kOutput, calls=%fused_computation.76 | convolution fusion | flops 3224369152 | bytes 20455424 | tf_op jit(solution)/shard_map/dot_general | solution.py:127
  314.5 5.1 fusion.94
  319.6 2.2 fusion.27
  323.5 5.5 fusion.84
  329.6 3.2 slice-done.2
  332.8 5.3 multiply_reduce_fusion.2
  338.1 27.2 %concatenate.42 = f32[4380,512]{1,0:T(8,128)} concatenate(f32[1536,512]{1,0:T(8,128)} %fusion.94, f32[1536,512]{1,0:T(8,128)S(1)} %fusion.95, f32[1282,512]{1,0:T(8,128)} %fusion.52, f32[1,512]{1,0:T(1,128)S(1)} %bitcast.156, f32[1,512]{1,0:T(1,128)S(1)} %bitcast.155, f32[1,512]{1,0:T(1,128)S(1)} %bitcast.154, f32[1,512]{1,0:T(1,128)S(1)} %bitcast.153, f32[1,512]{1,0:T(1,128)S(1)} %bitcast.152, ...), dimensions={0} | concatenate | bytes 17940480 | tf_op jit(solution)/shard_map/concatenate | solution.py:316
  365.4 8.1 %pad.35 = f32[4384,512]{1,0:T(8,128)} pad(f32[4380,512]{1,0:T(8,128)} %concatenate.42, f32[]{:T(128)} %constant.186.clone.1), padding=0_4x0_0 | pad | bytes 17948676 | tf_op jit(solution)/shard_map/jit(_pad)/pad | solution.py:319
  375.2 13.5 %fusion.6 = f32[2048,1280]{0,1:T(8,128)} fusion(bf16[2048,641]{0,1:T(8,128)(2,1)} %get-tuple-element.43, bf16[2048,641]{0,1:T(8,128)(2,1)S(1)} %copy-done.15, bf16[641,1280]{1,0:T(8,128)(2,1)} %get-tuple-element.93, bf16[641,1280]{1,0:T(8,128)(2,1)} %get-tuple-element.94), kind=kOutput, calls=%fused_computation.34 | convolution fusion | flops 6738438144 | bytes 19018752 | tf_op jit(solution)/shard_map/dot_general | solution.py:127
  388.7 14.4 %reshape.268 = f32[2,1024,4,320]{1,0,3,2:T(2,128)} reshape(f32[2048,1280]{0,1:T(8,128)} %fusion.6) | data formatting | bytes 20971520 | tf_op jit(solution)/shard_map/reshape | solution.py:212
  403.2 8.6 %copy_multiply_fusion = f32[2,1024,4,320]{1,3,0,2:T(8,128)S(1)} fusion(f32[2,1024,4,320]{1,0,3,2:T(2,128)} %reshape.268, f32[4,320]{1,0:T(4,128)S(1)} %copy-done.52), kind=kLoop, calls=%fused_computation.21 | loop fusion | flops 2621440 | bytes 20976640 | tf_op jit(solution)/shard_map/mul | solution.py:212
  415.8 2.3 pad_add_fusion
  420.2 4.7 collective-permute-start.12
  425.0 2.4 fusion.43
  427.5 2.3 copy.30
  429.8 4.1 reshape.269
  434.0 20.7 %fusion.13 = f32[2,1024,512]{2,1,0:T(8,128)} fusion(f32[2,3,512]{2,1,0:T(4,128)S(1)} %collective-permute-done.12, f32[2,3,512]{2,1,0:T(4,128)S(1)} %collective-permute-done.11, f32[2,1024,512]{2,1,0:T(8,128)} %bitcast.119, f32[2,1024,512]{2,1,0:T(8,128)} %bitcast.118, f32[512]{0:T(512)S(1)} %bitcast.135, f32[2,1024]{1,0:T(2,128)S(1)} %copy-done.31, ...), kind=kLoop, calls=%fused_computation.46 | loop fusion | flops 27262976 | bytes 12670976 | tf_op jit(solution)/shard_map/add | solution.py:302
  454.6 107.6 %all-reduce.10.cloned.1.call-done = f32[137,32,512]{2,1,0:T(8,128)} async-done(((f32[137,32,512]{2,1,0:T(8,128)}), f32[137,32,512]{2,1,0:T(8,128)}) %all-reduce.10.cloned.1.call-update) | async-done | bytes 8978448 | tf_op jit(solution)/shard_map/psum | solution.py:321
  562.2 9.1 %concatenate.43 = f32[138,32,512]{2,1,0:T(8,128)} pad(f32[137,32,512]{2,1,0:T(8,128)} %all-reduce.10.cloned.1.call-done, f32[]{:T(128)} %constant.186.clone.1), padding=0_1x0_0x0_0 | pad | bytes 18022404 | tf_op jit(solution)/shard_map/concatenate | solution.py:322
  571.3 4.5 gather_fusion.1
  575.8 5.5 multiply_subtract_fusion
  (243 shorter events, 35.2 us)
Async XLA Ops:
  7.2 555.0 %all-reduce.10.cloned.1.call-start = ((), (), s32[]{:S(2)}) async-start(), calls=%async_computation | async-start | bytes 17956864 | tf_op jit(solution)/shard_map/psum | solution.py:321
  7.2 15.4 %copy-start.70 = (s32[2,4]{1,0:T(2,128)S(1)}, s32[2,4]{1,0:T(2,128)}, u32[]{:S(2)}) copy-start(s32[2,4]{1,0:T(2,128)} %param.9) | copy-start | bytes 100
  12.5 41.1 %collective-permute-start = (bf16[27,32,512]{2,1,0:T(8,128)(2,1)}, bf16[27,32,512]{2,1,0:T(8,128)(2,1)}, u32[]{:S(2)}, u32[]{:S(2)}) collective-permute-start(bf16[27,32,512]{2,1,0:T(8,128)(2,1)} %get-tuple-element.39), channel_id=1, source_target_pairs={{0,4},{4,8},{8,12},{12,16},{16,20},{20,24},{24,28},{28,0},{1,5},{5... | collective-permute-start | bytes 2654216 | tf_op jit(solution)/shard_map/ppermute | solution.py:41
  15.4 70.1 %collective-permute-start.1 = (bf16[27,32,512]{2,1,0:T(8,128)(2,1)}, bf16[27,32,512]{2,1,0:T(8,128)(2,1)}, u32[]{:S(2)}, u32[]{:S(2)}) collective-permute-start(bf16[27,32,512]{2,1,0:T(8,128)(2,1)} %get-tuple-element.39), channel_id=1, source_target_pairs={{0,28},{4,0},{8,4},{12,8},{16,12},{20,16},{24,20},{28,24},{1,29},{... | collective-permute-start | bytes 2654216 | tf_op jit(solution)/shard_map/ppermute | solution.py:46
  19.8 53.8 %collective-permute-start.7 = (bf16[2,3,512]{2,1,0:T(4,128)(2,1)}, bf16[2,3,512]{2,1,0:T(4,128)(2,1)S(1)}, u32[]{:S(2)}, u32[]{:S(2)}) collective-permute-start(bf16[2,3,512]{2,1,0:T(4,128)(2,1)} %get-tuple-element.57), channel_id=1, source_target_pairs={{0,1},{1,2},{2,3},{4,5},{5,6},{6,7},{8,9},{9,10},{10,11},{12,13},{... | collective-permute-start | bytes 18440 | tf_op jit(solution)/shard_map/ppermute | solution.py:59
  21.2 52.3 %collective-permute-start.8 = (bf16[2,3,512]{2,1,0:T(4,128)(2,1)S(1)}, bf16[2,3,512]{2,1,0:T(4,128)(2,1)S(1)}, u32[]{:S(2)}, u32[]{:S(2)}) collective-permute-start(bf16[2,3,512]{2,1,0:T(4,128)(2,1)S(1)} %get-tuple-element.56), channel_id=1, source_target_pairs={{1,0},{2,1},{3,2},{5,4},{6,5},{7,6},{9,8},{10,9},{11,10},{13,12},{... | collective-permute-start | bytes 18440 | tf_op jit(solution)/shard_map/ppermute | solution.py:62
  23.0 158.7 %copy-start.24 = (f32[2,1024]{1,0:T(2,128)}, f32[2,1024]{1,0:T(2,128)S(1)}, u32[]{:S(2)}) copy-start(f32[2,1024]{1,0:T(2,128)S(1)} %get-tuple-element.70) | copy-start | bytes 24580
  23.0 158.7 %copy-start.26 = (f32[2,1024]{1,0:T(2,128)}, f32[2,1024]{1,0:T(2,128)S(1)}, u32[]{:S(2)}) copy-start(f32[2,1024]{1,0:T(2,128)S(1)} %get-tuple-element.74) | copy-start | bytes 24580
  23.1 158.7 %copy-start.28 = (f32[2,1024]{1,0:T(2,128)}, f32[2,1024]{1,0:T(2,128)S(1)}, u32[]{:S(2)}) copy-start(f32[2,1024]{1,0:T(2,128)S(1)} %get-tuple-element.75) | copy-start | bytes 24580
  23.1 158.7 %copy-start.30 = (f32[2,1024]{1,0:T(2,128)}, f32[2,1024]{1,0:T(2,128)S(1)}, u32[]{:S(2)}) copy-start(f32[2,1024]{1,0:T(2,128)S(1)} %get-tuple-element.71) | copy-start | bytes 24580
  23.1 158.7 %copy-start.32 = (f32[2,1024]{1,0:T(2,128)}, f32[2,1024]{1,0:T(2,128)S(1)}, u32[]{:S(2)}) copy-start(f32[2,1024]{1,0:T(2,128)S(1)} %get-tuple-element.72) | copy-start | bytes 24580
  23.1 158.7 %copy-start.34 = (f32[2,1024]{1,0:T(2,128)}, f32[2,1024]{1,0:T(2,128)S(1)}, u32[]{:S(2)}) copy-start(f32[2,1024]{1,0:T(2,128)S(1)} %get-tuple-element.73) | copy-start | bytes 24580
  23.2 16.4 %copy-start.44 = (f32[320]{0:T(512)}, f32[320]{0:T(512)S(1)}, u32[]{:S(2)}) copy-start(f32[320]{0:T(512)S(1)} %get-tuple-element.77) | copy-start | bytes 3844
  23.2 16.4 %copy-start.46 = (f32[320]{0:T(512)}, f32[320]{0:T(512)S(1)}, u32[]{:S(2)}) copy-start(f32[320]{0:T(512)S(1)} %get-tuple-element.78) | copy-start | bytes 3844
  23.2 16.4 %copy-start.48 = (f32[320]{0:T(512)}, f32[320]{0:T(512)S(1)}, u32[]{:S(2)}) copy-start(f32[320]{0:T(512)S(1)} %get-tuple-element.79) | copy-start | bytes 3844
  23.2 16.4 %copy-start.50 = (f32[320]{0:T(512)}, f32[320]{0:T(512)S(1)}, u32[]{:S(2)}) copy-start(f32[320]{0:T(512)S(1)} %get-tuple-element.80) | copy-start | bytes 3844
  28.1 4.9 copy-start.67
  31.7 57.1 %collective-permute-start.10 = (f32[2,3,320]{1,2,0:T(8,128)}, f32[2,3,320]{1,2,0:T(8,128)}, u32[]{:S(2)}, u32[]{:S(2)}) collective-permute-start(f32[2,3,320]{1,2,0:T(8,128)} %slice.387), channel_id=1, source_target_pairs={{1,0},{2,1},{3,2},{5,4},{6,5},{7,6},{9,8},{10,9},{11,10},{13,12},{... | collective-permute-start | bytes 23048 | tf_op jit(solution)/shard_map/ppermute | solution.py:70
  39.4 33.8 %copy-start.68 = (pred[137]{0:T(512)(128)(4,1)S(1)}, pred[137]{0:T(512)(128)(4,1)}, u32[]{:S(2)}) copy-start(pred[137]{0:T(512)(128)(4,1)} %get-tuple-element.36) | copy-start | bytes 415
  53.6 34.9 %collective-permute-start.2 = (bf16[27,32,512]{2,1,0:T(8,128)(2,1)}, bf16[27,32,512]{2,1,0:T(8,128)(2,1)}, u32[]{:S(2)}, u32[]{:S(2)}) collective-permute-start(bf16[27,32,512]{2,1,0:T(8,128)(2,1)} %collective-permute-done), channel_id=1, source_target_pairs={{0,4},{4,8},{8,12},{12,16},{16,20},{20,24},{24,28},{28,0},{1,5},{5... | collective-permute-start | bytes 2654216 | tf_op jit(solution)/shard_map/ppermute | solution.py:41
  73.5 121.5 %copy-start.36 = (s32[1,8,2,128]{3,1,2,0:T(8,128)}, s32[1,8,2,128]{3,1,2,0:T(8,128)S(1)}, u32[]{:S(2)}) copy-start(s32[1,8,2,128]{3,1,2,0:T(8,128)S(1)} %copy.47) | copy-start | bytes 24580
  82.9 5.8 copy-start.10
  85.5 39.4 %collective-permute-start.3 = (bf16[27,32,512]{2,1,0:T(8,128)(2,1)}, bf16[27,32,512]{2,1,0:T(8,128)(2,1)S(1)}, u32[]{:S(2)}, u32[]{:S(2)}) collective-permute-start(bf16[27,32,512]{2,1,0:T(8,128)(2,1)} %collective-permute-done.1), channel_id=1, source_target_pairs={{0,28},{4,0},{8,4},{12,8},{16,12},{20,16},{24,20},{28,24},{1,29},{... | collective-permute-start | bytes 2654216 | tf_op jit(solution)/shard_map/ppermute | solution.py:46
  88.5 39.1 %collective-permute-start.4 = (bf16[27,32,512]{2,1,0:T(8,128)(2,1)}, bf16[27,32,512]{2,1,0:T(8,128)(2,1)S(1)}, u32[]{:S(2)}, u32[]{:S(2)}) collective-permute-start(bf16[27,32,512]{2,1,0:T(8,128)(2,1)} %collective-permute-done.2), channel_id=1, source_target_pairs={{0,4},{4,8},{8,12},{12,16},{16,20},{20,24},{24,28},{28,0},{1,5},{5... | collective-permute-start | bytes 2654216 | tf_op jit(solution)/shard_map/ppermute | solution.py:41
  106.6 21.4 %copy-start.20 = (bf16[641,1280]{1,0:T(8,128)(2,1)S(1)}, bf16[641,1280]{1,0:T(8,128)(2,1)}, u32[]{:S(2)}) copy-start(bf16[641,1280]{1,0:T(8,128)(2,1)} %get-tuple-element.93) | copy-start | bytes 4922884
  106.6 21.4 %copy-start.21 = (bf16[641,1280]{1,0:T(8,128)(2,1)S(1)}, bf16[641,1280]{1,0:T(8,128)(2,1)}, u32[]{:S(2)}) copy-start(bf16[641,1280]{1,0:T(8,128)(2,1)} %get-tuple-element.94) | copy-start | bytes 4922884
  124.9 38.3 %collective-permute-start.5 = (bf16[27,32,512]{2,1,0:T(8,128)(2,1)S(1)}, bf16[27,32,512]{2,1,0:T(8,128)(2,1)S(1)}, u32[]{:S(2)}, u32[]{:S(2)}) collective-permute-start(bf16[27,32,512]{2,1,0:T(8,128)(2,1)S(1)} %collective-permute-done.3), channel_id=1, source_target_pairs={{0,28},{4,0},{8,4},{12,8},{16,12},{20,16},{24,20},{28,24},{1,29},{... | collective-permute-start | bytes 2654216 | tf_op jit(solution)/shard_map/ppermute | solution.py:46
  127.6 36.6 %collective-permute-start.6 = (bf16[27,32,512]{2,1,0:T(8,128)(2,1)S(1)}, bf16[27,32,512]{2,1,0:T(8,128)(2,1)S(1)}, u32[]{:S(2)}, u32[]{:S(2)}) collective-permute-start(bf16[27,32,512]{2,1,0:T(8,128)(2,1)S(1)} %collective-permute-done.4), channel_id=1, source_target_pairs={{0,4},{4,8},{8,12},{12,16},{16,20},{20,24},{24,28},{28,0},{1,5},{5... | collective-permute-start | bytes 2654216 | tf_op jit(solution)/shard_map/ppermute | solution.py:41
  165.1 10.5 %copy-start.69 = (pred[137]{0:T(512)(128)(4,1)S(1)}, pred[137]{0:T(512)(128)(4,1)}, u32[]{:S(2)}) copy-start(pred[137]{0:T(512)(128)(4,1)} %get-tuple-element.36) | copy-start | bytes 415
  175.7 6.1 %slice-start = ((s8[4227072]{0:T(1024)(128)(4,1)}), s8[32768]{0:T(1024)(128)(4,1)S(1)}, s32[]{:S(2)}) async-start(s8[4227072]{0:T(1024)(128)(4,1)} %bitcast.113), calls=%async_computation.1 | async-start | bytes 65536
  181.6 10.6 %copy-start.13 = (bf16[4384,512]{1,0:T(8,128)(2,1)}, bf16[4384,512]{1,0:T(8,128)(2,1)S(1)}, u32[]{:S(2)}) copy-start(bf16[4384,512]{1,0:T(8,128)(2,1)S(1)} %bitcast_select_fusion) | copy-start | bytes 13467652
  181.6 6.2 %copy-start.53 = (f32[1,512]{1,0:T(1,128)}, f32[1,512]{1,0:T(1,128)S(1)}, u32[]{:S(2)}) copy-start(f32[1,512]{1,0:T(1,128)S(1)} %get-tuple-element.61) | copy-start | bytes 6148
  181.6 6.2 %copy-start.55 = (f32[1,512]{1,0:T(1,128)}, f32[1,512]{1,0:T(1,128)S(1)}, u32[]{:S(2)}) copy-start(f32[1,512]{1,0:T(1,128)S(1)} %get-tuple-element.62) | copy-start | bytes 6148
  181.7 6.2 %copy-start.57 = (f32[1,512]{1,0:T(1,128)}, f32[1,512]{1,0:T(1,128)S(1)}, u32[]{:S(2)}) copy-start(f32[1,512]{1,0:T(1,128)S(1)} %get-tuple-element.63) | copy-start | bytes 6148
  181.7 6.2 %copy-start.59 = (f32[1,512]{1,0:T(1,128)}, f32[1,512]{1,0:T(1,128)S(1)}, u32[]{:S(2)}) copy-start(f32[1,512]{1,0:T(1,128)S(1)} %get-tuple-element.64) | copy-start | bytes 6148
  181.7 6.2 %copy-start.61 = (f32[1,512]{1,0:T(1,128)}, f32[1,512]{1,0:T(1,128)S(1)}, u32[]{:S(2)}) copy-start(f32[1,512]{1,0:T(1,128)S(1)} %get-tuple-element.65) | copy-start | bytes 6148
  181.7 6.2 %copy-start.63 = (f32[1,512]{1,0:T(1,128)}, f32[1,512]{1,0:T(1,128)S(1)}, u32[]{:S(2)}) copy-start(f32[1,512]{1,0:T(1,128)S(1)} %get-tuple-element.66) | copy-start | bytes 6148
  181.7 6.2 %copy-start.65 = (f32[1,512]{1,0:T(1,128)}, f32[1,512]{1,0:T(1,128)S(1)}, u32[]{:S(2)}) copy-start(f32[1,512]{1,0:T(1,128)S(1)} %get-tuple-element.67) | copy-start | bytes 6148
  189.8 5.1 copy-start.38
  194.9 5.2 copy-start.22
  194.9 36.8 %copy-start.23 = (bf16[48,32,512]{2,1,0:T(8,128)(2,1)}, bf16[48,32,512]{2,1,0:T(8,128)(2,1)S(1)}, u32[]{:S(2)}) copy-start(bf16[48,32,512]{2,1,0:T(8,128)(2,1)S(1)} %get-tuple-element.47) | copy-start | bytes 4718596
  200.1 31.6 %copy-start.17 = (bf16[2048,512]{1,0:T(8,128)(2,1)}, bf16[2048,512]{1,0:T(8,128)(2,1)S(1)}, u32[]{:S(2)}) copy-start(bf16[2048,512]{1,0:T(8,128)(2,1)S(1)} %add_convert_fusion.3) | copy-start | bytes 6291460
  200.1 31.6 %copy-start.16 = (bf16[2,1024,512]{2,1,0:T(8,128)(2,1)S(1)}, bf16[2,1024,512]{2,1,0:T(8,128)(2,1)}, u32[]{:S(2)}) copy-start(bf16[2,1024,512]{2,1,0:T(8,128)(2,1)} %param.8) | copy-start | bytes 6291460
  231.8 5.4 copy-start.73
  286.3 5.2 copy-start.4
  287.0 4.5 copy-start.19
  291.5 16.5 %copy-start.3 = (f32[2048,512]{1,0:T(8,128)S(1)}, f32[2048,512]{1,0:T(8,128)}, u32[]{:S(2)}) copy-start(f32[2048,512]{1,0:T(8,128)} %bitcast_subtract_fusion) | copy-start | bytes 12582916
  291.5 16.5 %copy-start.5 = (f32[2048,512]{1,0:T(8,128)S(1)}, f32[2048,512]{1,0:T(8,128)}, u32[]{:S(2)}) copy-start(f32[2048,512]{1,0:T(8,128)} %fusion.60) | copy-start | bytes 12582916
  308.0 6.5 %copy-start.18 = (bf16[2048,512]{1,0:T(8,128)(2,1)S(1)}, bf16[2048,512]{1,0:T(8,128)(2,1)}, u32[]{:S(2)}) copy-start(bf16[2048,512]{1,0:T(8,128)(2,1)} %copy-done.17) | copy-start | bytes 6291460
  308.0 6.5 %copy-start.72 = (bf16[2048,1536]{1,0:T(8,128)(2,1)S(1)}, bf16[2048,1536]{1,0:T(8,128)(2,1)}, u32[]{:S(2)}) copy-start(bf16[2048,1536]{1,0:T(8,128)(2,1)} %get-tuple-element.92) | copy-start | bytes 18874372
  314.4 7.3 %copy-start.6 = (f32[2048,512]{1,0:T(8,128)}, f32[2048,512]{1,0:T(8,128)S(1)}, u32[]{:S(2)}) copy-start(f32[2048,512]{1,0:T(8,128)S(1)} %get-tuple-element.90) | copy-start | bytes 12582916
  314.5 5.1 copy-start.37
  314.5 5.1 copy-start.39
  329.6 8.6 %copy-start.2 = (f32[2048,512]{1,0:T(8,128)}, f32[2048,512]{1,0:T(8,128)S(1)}, u32[]{:S(2)}) copy-start(f32[2048,512]{1,0:T(8,128)S(1)} %get-tuple-element.25) | copy-start | bytes 12582916
  388.7 14.4 %copy-start.52 = (f32[4,320]{1,0:T(4,128)S(1)}, f32[4,320]{1,0:T(4,128)}, u32[]{:S(2)}) copy-start(f32[4,320]{1,0:T(4,128)} %multiply_subtract_fusion.2) | copy-start | bytes 15364
  414.2 10.8 %copy-start.45 = (f32[320]{0:T(512)S(1)}, f32[320]{0:T(512)}, u32[]{:S(2)}) copy-start(f32[320]{0:T(512)} %copy-done.44) | copy-start | bytes 3844
  414.2 10.8 %copy-start.47 = (f32[320]{0:T(512)S(1)}, f32[320]{0:T(512)}, u32[]{:S(2)}) copy-start(f32[320]{0:T(512)} %copy-done.46) | copy-start | bytes 3844
  414.2 10.8 %copy-start.49 = (f32[320]{0:T(512)S(1)}, f32[320]{0:T(512)}, u32[]{:S(2)}) copy-start(f32[320]{0:T(512)} %copy-done.48) | copy-start | bytes 3844
  414.2 10.8 %copy-start.51 = (f32[320]{0:T(512)S(1)}, f32[320]{0:T(512)}, u32[]{:S(2)}) copy-start(f32[320]{0:T(512)} %copy-done.50) | copy-start | bytes 3844
  414.2 10.7 %collective-permute-start.9 = (f32[2,3,320]{1,2,0:T(8,128)S(1)}, f32[2,3,320]{1,2,0:T(8,128)S(1)}, u32[]{:S(2)}, u32[]{:S(2)}) collective-permute-start(f32[2,3,320]{1,2,0:T(8,128)S(1)} %pad_add_fusion.1), channel_id=1, source_target_pairs={{0,1},{1,2},{2,3},{4,5},{5,6},{6,7},{8,9},{9,10},{10,11},{12,13},{... | collective-permute-start | bytes 23048 | tf_op jit(solution)/shard_map/ppermute | solution.py:70
  419.0 14.9 %collective-permute-start.11 = (f32[2,3,512]{2,1,0:T(4,128)S(1)}, f32[2,3,512]{2,1,0:T(4,128)S(1)}, u32[]{:S(2)}, u32[]{:S(2)}) collective-permute-start(f32[2,3,512]{2,1,0:T(4,128)S(1)} %get-tuple-element.51), channel_id=1, source_target_pairs={{1,0},{2,1},{3,2},{5,4},{6,5},{7,6},{9,8},{10,9},{11,10},{13,12},{... | collective-permute-start | bytes 36872 | tf_op jit(solution)/shard_map/ppermute | solution.py:62
  420.2 13.7 %collective-permute-start.12 = (f32[2,3,512]{2,1,0:T(4,128)S(1)}, f32[2,3,512]{2,1,0:T(4,128)S(1)}, u32[]{:S(2)}, u32[]{:S(2)}) collective-permute-start(f32[2,3,512]{2,1,0:T(4,128)S(1)} %get-tuple-element.52), channel_id=1, source_target_pairs={{0,1},{1,2},{2,3},{4,5},{5,6},{6,7},{8,9},{9,10},{10,11},{12,13},{... | collective-permute-start | bytes 36872 | tf_op jit(solution)/shard_map/ppermute | solution.py:59
  454.6 121.2 %copy-start.71 = (pred[27]{0:T(512)(128)(4,1)S(1)}, pred[27]{0:T(512)(128)(4,1)}, u32[]{:S(2)}) copy-start(pred[27]{0:T(512)(128)(4,1)} %get-tuple-element.18) | copy-start | bytes 85
  571.3 4.5 copy-start.12
  (30 other events, 97.4 us)
Sparse Core Ops, SparseCore 0:
  373.6 188.5 all-reduce.9
